TPU v7x, 32 devices: a whole 2x2x4 slice. The times are simulated.
32 devices in a mesh: row: 4 (over y, core), col: 8 (over z, x).
Axes of the slice: x: 2, y: 2, z: 4, core: 2. Of those that a mesh axis runs over, the one named last changes fastest.
Arguments:
- slab: float32 [16384, 8192], P(('row', 'col')), may hold values from -80 to 80, as said below
- sketch: float32 [8192, 128], replicated, may hold values from -0.0625 to 0.0625
Outputs:
- basis: float32 [16384, 128], P(('row', 'col'))
- projection: float32 [128, 8192], replicated
Inputs may be any that keep to these rules, and one draw needn't show every extreme that they name: `slab`: each entry is one hidden-state value.
All inputs are finite; a program needn't handle non-finite values.
Results may differ from a plain program's by a relative error of at most 0.000084.
Values sent between devices are 32-bit elements; how exact they have to be, the bound alone decides.
A program may use at most 128 MiB of HBM per device.

v0:
```python
import math

import jax
import jax.numpy as jnp
from jax import lax
from jax.sharding import PartitionSpec as P


def from_partner(value, axis, apart):
    mask = 2**apart
    pairs = [(source, source ^ mask) for source in range(lax.axis_size(axis))]
    return lax.ppermute(value, axis, pairs)


def merge_level(lower, partner):
    highest = lax.Precision.HIGHEST
    combined = jnp.dot(lower, lower.T, precision=highest) + jnp.dot(
        partner, partner.T, precision=highest
    )
    return jnp.linalg.cholesky(combined)


def row_levels(lower):
    for bit in range(lax.axis_size("row").bit_length() - 1):
        lower = merge_level(lower, from_partner(lower, "row", bit))
    return lower


def col_levels(lower):
    for bit in range(lax.axis_size("col").bit_length() - 1):
        lower = merge_level(lower, from_partner(lower, "col", bit))
    return lower


def per_device(slab, sketch):
    highest = lax.Precision.HIGHEST
    sampled = jnp.dot(slab, sketch, precision=highest, preferred_element_type=jnp.float32)
    local_gram = jnp.dot(sampled.T, sampled, precision=highest)
    lower = jnp.linalg.cholesky(local_gram)
    lower = col_levels(row_levels(lower))
    transposed = jax.scipy.linalg.solve_triangular(lower, sampled.T, lower=True)
    total_rows = slab.shape[0] * lax.axis_size("row") * lax.axis_size("col")
    basis = transposed.T * math.sqrt(total_rows)
    projection = lax.psum(jnp.dot(transposed, slab, precision=highest), ("row", "col"))
    return (basis, projection)


def solution(mesh):
    placed = (P(("row", "col"), None), P())
    return jax.shard_map(
        per_device,
        mesh=mesh,
        in_specs=placed,
        out_specs=(P(("row", "col"), None), P()),
        check_vma=False,
    )
```

profile of v0, /device:TPU:1, one launch (start us, length us, event | category | flops | bytes accessed | tf_op | source)
XLA Modules:
  0.0 303.2 jit_solution(1789928694938599340)
XLA Ops:
  7.2 16.4 %fusion.19 = f32[512,128]{1,0:T(8,128)S(1)} fusion(f32[512,8192]{1,0:T(8,128)} %param.3, f32[8192,128]{1,0:T(8,128)} %param.4), kind=kOutput, calls=%fused_computation.46 | convolution fusion | flops 6442450944 | bytes 21233664 | tf_op jit(solution)/shard_map/dot_general | solution.py:37
  24.3 11.7 %cholesky.104 = f32[128,128]{1,0:T(8,128)S(1)} custom-call(f32[128,128]{1,0:T(8,128)S(1)} %fusion.8), custom_call_target="Cholesky" | custom-call | tf_op jit(solution)/shard_map/jit(cholesky)/cholesky | solution.py:39
  36.1 0.6 compare_reduce_fusion.5
  36.7 0.7 select_select_fusion.5
  37.8 0.9 collective-permute-done
  39.1 11.7 %cholesky.115 = f32[128,128]{1,0:T(8,128)S(1)} custom-call(f32[128,128]{1,0:T(8,128)S(1)} %fusion.7), custom_call_target="Cholesky" | custom-call | tf_op jit(solution)/shard_map/jit(cholesky)/cholesky | solution.py:20
  50.8 0.6 compare_reduce_fusion.4
  51.5 0.7 select_select_fusion.4
  52.1 2.5 collective-permute-start.1
  54.8 1.9 collective-permute-done.1
  57.1 11.9 %cholesky.126 = f32[128,128]{1,0:T(8,128)S(1)} custom-call(f32[128,128]{1,0:T(8,128)S(1)} %fusion.6), custom_call_target="Cholesky" | custom-call | tf_op jit(solution)/shard_map/jit(cholesky)/cholesky | solution.py:20
  69.1 0.6 compare_reduce_fusion.3
  69.7 0.7 select_select_fusion.3
  70.4 1.0 collective-permute-start.2
  71.6 1.9 collective-permute-done.2
  74.0 11.7 %cholesky.137 = f32[128,128]{1,0:T(8,128)S(1)} custom-call(f32[128,128]{1,0:T(8,128)S(1)} %fusion.5), custom_call_target="Cholesky" | custom-call | tf_op jit(solution)/shard_map/jit(cholesky)/cholesky | solution.py:20
  85.7 0.6 compare_reduce_fusion.2
  86.4 0.7 select_select_fusion.2
  87.0 1.1 collective-permute-start.3
  88.3 1.9 collective-permute-done.3
  90.6 11.7 %cholesky.148 = f32[128,128]{1,0:T(8,128)S(1)} custom-call(f32[128,128]{1,0:T(8,128)S(1)} %fusion.4), custom_call_target="Cholesky" | custom-call | tf_op jit(solution)/shard_map/jit(cholesky)/cholesky | solution.py:20
  102.3 0.6 compare_reduce_fusion.1
  103.0 0.7 select_select_fusion.1
  103.6 2.1 collective-permute-start.4
  106.0 1.7 collective-permute-done.4
  108.1 12.0 %cholesky.159 = f32[128,128]{1,0:T(8,128)S(1)} custom-call(f32[128,128]{1,0:T(8,128)S(1)} %fusion.3), custom_call_target="Cholesky" | custom-call | tf_op jit(solution)/shard_map/jit(cholesky)/cholesky | solution.py:20
  120.7 0.7 fusion
  121.4 9.8 %custom-call.6 = f32[1,128,128]{1,2,0:T(8,128)S(1)} custom-call(f32[1,128,128]{2,1,0:T(8,128)S(1)} %fusion), custom_call_target="InvertDiagBlocksLowerTriangular" | custom-call | tf_op jit(solution)/shard_map/jit(_solve_triangular)/triangular_solve | solution.py:41
  131.7 13.8 %fusion.26 = f32[128,8192]{1,0:T(8,128)} fusion(f32[128,512]{1,0:T(8,128)S(1)} %fusion.1, f32[512,8192]{1,0:T(8,128)} %param.3), kind=kOutput, calls=%fused_computation.53 | convolution fusion | flops 6442450944 | bytes 21233664 | tf_op jit(solution)/shard_map/dot_general | solution.py:44
  145.5 0.8 copy.20
  146.3 145.0 %all-reduce.2.cloned.1.call-done = f32[128,8192]{1,0:T(8,128)} async-done(((f32[128,8192]{1,0:T(8,128)}), f32[128,8192]{1,0:T(8,128)}) %all-reduce.2.cloned.1.call-update) | async-done | bytes 4194320 | tf_op jit(solution)/shard_map/psum | solution.py:44
  291.3 4.6 %copy.32 = f32[128,8192]{1,0:T(8,128)} copy(f32[128,8192]{1,0:T(8,128)} %all-reduce.2.cloned.1.call-done) | data formatting | bytes 8388608
  (35 shorter events, 5.3 us)
Async XLA Ops:
  7.2 284.2 %all-reduce.2.cloned.1.call-start = ((), (), s32[]{:S(2)}) async-start(), calls=%async_computation | async-start | bytes 8388608 | tf_op jit(solution)/shard_map/psum | solution.py:44
  37.4 1.3 collective-permute-start
  52.1 4.6 %collective-permute-start.1 = (f32[128,128]{1,0:T(8,128)S(1)}, f32[128,128]{1,0:T(8,128)S(1)}, u32[]{:S(2)}, u32[]{:S(2)}) collective-permute-start(f32[128,128]{1,0:T(8,128)S(1)} %select_select_fusion.4), channel_id=1, source_target_pairs={{0,16},{8,24},{16,0},{24,8},{1,17},{9,25},{17,1},{25,9},{2,18},{10... | collective-permute-start | bytes 196616 | tf_op jit(solution)/shard_map/ppermute | solution.py:12
  70.4 3.2 %collective-permute-start.2 = (f32[128,128]{1,0:T(8,128)S(1)}, f32[128,128]{1,0:T(8,128)S(1)}, u32[]{:S(2)}, u32[]{:S(2)}) collective-permute-start(f32[128,128]{1,0:T(8,128)S(1)} %select_select_fusion.3), channel_id=1, source_target_pairs={{0,1},{1,0},{2,3},{3,2},{4,5},{5,4},{6,7},{7,6},{8,9},{9,8},{10,11... | collective-permute-start | bytes 196616 | tf_op jit(solution)/shard_map/ppermute | solution.py:12
  87.0 3.2 %collective-permute-start.3 = (f32[128,128]{1,0:T(8,128)S(1)}, f32[128,128]{1,0:T(8,128)S(1)}, u32[]{:S(2)}, u32[]{:S(2)}) collective-permute-start(f32[128,128]{1,0:T(8,128)S(1)} %select_select_fusion.2), channel_id=1, source_target_pairs={{0,2},{1,3},{2,0},{3,1},{4,6},{5,7},{6,4},{7,5},{8,10},{9,11},{10,... | collective-permute-start | bytes 196616 | tf_op jit(solution)/shard_map/ppermute | solution.py:12
  103.6 4.1 %collective-permute-start.4 = (f32[128,128]{1,0:T(8,128)S(1)}, f32[128,128]{1,0:T(8,128)S(1)}, u32[]{:S(2)}, u32[]{:S(2)}) collective-permute-start(f32[128,128]{1,0:T(8,128)S(1)} %select_select_fusion.1), channel_id=1, source_target_pairs={{0,4},{1,5},{2,6},{3,7},{4,0},{5,1},{6,2},{7,3},{8,12},{9,13},{10,... | collective-permute-start | bytes 196616 | tf_op jit(solution)/shard_map/ppermute | solution.py:12
Sparse Core Ops, SparseCore 0:
  145.6 145.7 all-reduce.1
where the time goes:
time: 309 us; the launch traced here: 303 us
  waiting for transfers between devices  153 us (50%)
  other arithmetic  88.6 us (29%)
  matrix products  33.8 us (11%)
  between operations  14.7 us (5%)
  starting transfers between devices  6.72 us (2%)
  local copies, waits for them, and re-layouts  5.99 us (2%)
    psum x1, waiting for transfers between devices, per_device(): lax.psum(jnp.dot(transposed, slab, precision=highest), ('row', 'col'))  145 us
    another operation x15, other arithmetic, merge_level(): return jnp.linalg.cholesky(combined)  62.4 us
    dot_general x1, matrix products, per_device(): jnp.dot(slab, sketch, precision=highest, preferred_element_type=jnp.float32)  16.4 us
    dot_general x1, matrix products, per_device(): jnp.dot(transposed, slab, precision=highest)  13.8 us
    another operation x3, other arithmetic, per_device(): lower = jnp.linalg.cholesky(local_gram)  12.4 us
    another operation x2, other arithmetic, per_device(): transposed = jax.scipy.linalg.solve_triangular(lower, sampled.T, lower=True)  10.5 us
    ppermute x5, waiting for transfers between devices, from_partner(): return lax.ppermute(value, axis, pairs)  8.41 us
    ppermute x5, starting transfers between devices, from_partner(): return lax.ppermute(value, axis, pairs)  6.68 us
  transfers between devices with their start and end apart: 6, of which 6 were waited for; matrix products, arithmetic and copies ran while one was open for 1% of the time, Pallas kernels for 0%

commit v1 on v0

v1 whole, which is shorter than its diff:
```python
import functools
import math

import jax
import jax.numpy as jnp
from jax import lax
from jax.experimental import pallas as pl
from jax.experimental.pallas import tpu as pltpu
from jax.sharding import PartitionSpec as P

MESH = pl.DeviceIdType.MESH
BF16 = jnp.bfloat16
F32 = jnp.float32
LANES = 128
TILE = 8
LOAD = 512
WIDE = 256
CHUNKS = 8
CHOL = 16


def split(value):
    high = value.astype(BF16)
    return high, (value - high.astype(F32)).astype(BF16)


def bit_of(axis, bit):
    index = lax.axis_index(axis)
    value = (index // 2**bit) % 2
    return {axis: 2**bit * (1 - 2 * value)}, value


def chunk_order(chunk, rows, cols):
    row_bits = [("row", b) for b in range(1, rows.bit_length() - 1)]
    col_bits = [("col", b) for b in range(cols.bit_length() - 1)]
    inner = 1 if len(col_bits) == 3 else len(col_bits) // 2
    near, far = col_bits[:inner], col_bits[inner:]
    core = [("row", 0)]
    if chunk % 3 == 2:
        return core + near + row_bits + far, core + row_bits + near + far
    return core + near + far + row_bits, core + row_bits + far + near


def pick(even, odd):
    core = lax.axis_index("row") % 2
    device = {"row": lax.axis_index("row"), "col": lax.axis_index("col")}
    bit = 0
    for (axis, place), weight in ((even, 1 - core), (odd, core)):
        step, value = bit_of(axis, place)
        device[axis] = device[axis] + weight * step[axis]
        bit = bit + weight * value
    return (device["row"], device["col"]), bit


def sum_kernel(
    rows, cols, slab, sketch, total_ref, sampled_ref, inverse_ref,
    staged, sk, high, low, part, landed, left, grams, gram_in, work, wide_acc, slab_sem, sk_sem,
    send_sem, recv_sem, gram_send, gram_recv,
):
    height, width = slab.shape
    bits = (rows * cols).bit_length() - 1
    units = width // LANES * (LANES // TILE)
    chunk_units = units // CHUNKS
    chunk_cols = width // CHUNKS
    loads = width // LOAD

    sketch_copy = pltpu.make_async_copy(sketch, sk, sk_sem)
    sketch_copy.start()

    def load(i):
        return pltpu.make_async_copy(
            slab.at[:, pl.ds(pl.multiple_of(i * LOAD, LOAD), LOAD)], staged.at[i], slab_sem.at[i]
        )

    for i in range(loads):
        load(i).start()

    orders = [chunk_order(k, rows, cols) for k in range(CHUNKS)]
    gram_order = [("row", 0)] + [b for b in orders[0][0] if b != ("row", 0)]
    barrier = pltpu.get_barrier_semaphore()
    for place in gram_order:
        device, _ = pick(place, place)
        pl.semaphore_signal(barrier, inc=1, device_id=device, device_id_type=MESH)

    wide_acc[...] = jnp.zeros_like(wide_acc)
    sketch_copy.wait()

    def sample(i, carry):
        load(i).wait()
        a_high, a_low = split(staged[i])
        columns = pl.ds(pl.multiple_of(i * LOAD, LOAD), LOAD)
        high[:, columns] = a_high
        low[:, columns] = a_low
        s_high, s_low = split(sk[columns, :])
        both = jnp.concatenate([s_high, s_low], axis=1)
        wide_acc[...] += jnp.dot(a_high, both, preferred_element_type=F32)
        wide_acc[:, :LANES] += jnp.dot(a_low, s_high, preferred_element_type=F32)
        return carry

    lax.fori_loop(0, loads, sample, 0)
    sampled = wide_acc[:, :LANES] + wide_acc[:, LANES:]
    sampled_ref[...] = sampled
    turned = sampled.T
    t_high, t_low = split(turned)
    left[:LANES, :] = t_high
    left[LANES:, :] = t_low
    grams[0] = jnp.dot(
        turned, sampled, precision=lax.Precision.HIGHEST, preferred_element_type=F32
    )
    pl.semaphore_wait(barrier, bits)

    def product(k):
        def body(i, carry):
            start = pl.multiple_of(k * chunk_cols + i * WIDE, WIDE)
            b_high = high[:, pl.ds(start, WIDE)]
            both = jnp.dot(left[...], b_high, preferred_element_type=F32)
            more = jnp.dot(left[:LANES, :], low[:, pl.ds(start, WIDE)], preferred_element_type=F32)
            value = both[:LANES] + both[LANES:] + more
            per = LANES // TILE
            first = (k * chunk_cols // LANES + i * (WIDE // LANES)) * per
            for j in range(WIDE // LANES):
                part[pl.ds(first + j * per, per)] = value[:, j * LANES : (j + 1) * LANES].reshape(
                    per, TILE, LANES
                )
            return carry

        lax.fori_loop(0, chunk_cols // WIDE, body, 0)

    plan = []
    for k in range(CHUNKS):
        start, size, steps = k * chunk_units, chunk_units, []
        for even, odd in zip(*orders[k]):
            device, bit = pick(even, odd)
            half = size // 2
            keep, give = start + bit * half, start + (1 - bit) * half
            steps.append((device, keep, give, half, k * chunk_units + chunk_units - size))
            start, size = keep, half
        plan.append(steps)

    def scatter(k, s):
        device, _, give, half, slot = plan[k][s]
        return pltpu.make_async_remote_copy(
            src_ref=part.at[pl.ds(give, half)],
            dst_ref=landed.at[pl.ds(slot, half)],
            send_sem=send_sem.at[k, s],
            recv_sem=recv_sem.at[k, s],
            device_id=device,
            device_id_type=MESH,
        )

    def gather(k, s):
        device, keep, _, half, _ = plan[k][s]
        return pltpu.make_async_remote_copy(
            src_ref=total_ref.at[pl.ds(keep, half)],
            dst_ref=total_ref.at[pl.ds(keep, half)],
            send_sem=send_sem.at[k, 2 * bits - 1 - s],
            recv_sem=recv_sem.at[k, 2 * bits - 1 - s],
            device_id=device,
            device_id_type=MESH,
        )

    def exchange_gram(s):
        device, _ = pick(gram_order[s], gram_order[s])
        return pltpu.make_async_remote_copy(
            src_ref=grams.at[s],
            dst_ref=gram_in.at[s],
            send_sem=gram_send.at[s],
            recv_sem=gram_recv.at[s],
            device_id=device,
            device_id_type=MESH,
        )

    def chunk_step(k, s):
        if s == 0:
            product(k)
            scatter(k, 0).start()
        elif s <= bits:
            scatter(k, s - 1).wait_recv()
            _, keep, _, half, slot = plan[k][s - 1]
            value = part[pl.ds(keep, half)] + landed[pl.ds(slot, half)]
            if s < bits:
                part[pl.ds(keep, half)] = value
                scatter(k, s).start()
            else:
                total_ref[pl.ds(keep, half)] = value
                gather(k, bits - 1).start()
        else:
            gather(k, 2 * bits - s).wait_recv()
            if s < 2 * bits:
                gather(k, 2 * bits - s - 1).start()

    def gram_step(t):
        if 1 <= t <= bits:
            exchange_gram(t - 1).wait_recv()
            grams[t] = grams[t - 1] + gram_in[t - 1]
        if t < bits:
            exchange_gram(t).start()
        if t == bits:
            work[:, :LANES] = grams[bits]
            work[:, LANES:] = (
                lax.broadcasted_iota(jnp.int32, (LANES, LANES), 0)
                == lax.broadcasted_iota(jnp.int32, (LANES, LANES), 1)
            ).astype(F32)
        first = (t - bits - 1) * CHOL
        if 0 <= first < LANES:
            eliminate(first)

    def eliminate(first):
        lane = lax.broadcasted_iota(jnp.int32, (LANES, LANES), 1)
        sub = lax.broadcasted_iota(jnp.int32, (LANES, 1), 0)

        def body(j, carry):
            all_rows = work[...]
            column = jnp.sum(jnp.where(lane == j, all_rows[:, :LANES], 0.0), axis=1, keepdims=True)
            row = work[pl.ds(j, 1), :]
            pivot = jnp.sum(jnp.where(sub == j, column, 0.0), axis=0, keepdims=True)
            scale = 1.0 / jnp.sqrt(pivot)
            row = row * scale
            below = jnp.where(sub > j, column * scale, 0.0)
            work[...] = jnp.where(sub == j, row, all_rows - below * row)
            return carry

        lax.fori_loop(first, first + CHOL, body, 0)

    for t in range(max(CHUNKS + 2 * bits, bits + 1 + LANES // CHOL)):
        gram_step(t)
        for k in range(CHUNKS):
            if 0 <= t - k <= 2 * bits:
                chunk_step(k, t - k)

    inverse_ref[...] = work[:, LANES:]
    for k in range(CHUNKS):
        for s in range(bits):
            scatter(k, s).wait_send()
            gather(k, s).wait_send()
    for s in range(bits):
        exchange_gram(s).wait_send()


def apply_kernel(scale, total_ref, sampled_ref, inverse_ref, basis_ref, projection_ref):
    highest = lax.Precision.HIGHEST
    inverse = inverse_ref[...]

    @pl.when(pl.program_id(0) == 0)
    def _():
        turned = lax.dot_general(
            sampled_ref[...], inverse, (((1,), (1,)), ((), ())),
            precision=highest, preferred_element_type=F32,
        )
        basis_ref[...] = turned * scale

    per = LANES // TILE
    blocks = total_ref.shape[0] // per
    value = jnp.concatenate(
        [total_ref[b * per : (b + 1) * per].reshape(LANES, LANES) for b in range(blocks)], axis=1
    )
    projection_ref[...] = jnp.dot(inverse, value, precision=highest, preferred_element_type=F32)


def per_device(rows, cols, slab, sketch):
    height, width = slab.shape
    rank = sketch.shape[1]
    bits = (rows * cols).bit_length() - 1
    units = width // LANES * (rank // TILE)
    vmem = pl.BlockSpec(memory_space=pltpu.VMEM)
    total, sampled, inverse = pl.pallas_call(
        functools.partial(sum_kernel, rows, cols),
        out_shape=(
            jax.ShapeDtypeStruct((units, TILE, LANES), F32),
            jax.ShapeDtypeStruct((height, rank), F32),
            jax.ShapeDtypeStruct((rank, rank), F32),
        ),
        in_specs=[pl.BlockSpec(memory_space=pl.ANY)] * 2,
        out_specs=(vmem, vmem, vmem),
        scratch_shapes=[
            pltpu.VMEM((width // LOAD, height, LOAD), F32),
            pltpu.VMEM((width, rank), F32),
            pltpu.VMEM((height, width), BF16),
            pltpu.VMEM((height, width), BF16),
            pltpu.VMEM((units, TILE, LANES), F32),
            pltpu.VMEM((units, TILE, LANES), F32),
            pltpu.VMEM((2 * rank, height), BF16),
            pltpu.VMEM((bits + 1, rank, rank), F32),
            pltpu.VMEM((bits, rank, rank), F32),
            pltpu.VMEM((rank, 2 * rank), F32),
            pltpu.VMEM((height, 2 * rank), F32),
            pltpu.SemaphoreType.DMA((width // LOAD,)),
            pltpu.SemaphoreType.DMA,
            pltpu.SemaphoreType.DMA((CHUNKS, 2 * bits)),
            pltpu.SemaphoreType.DMA((CHUNKS, 2 * bits)),
            pltpu.SemaphoreType.DMA((bits,)),
            pltpu.SemaphoreType.DMA((bits,)),
        ],
        compiler_params=pltpu.CompilerParams(
            collective_id=0, has_side_effects=True, vmem_limit_bytes=56 * 2**20
        ),
    )(slab, sketch)
    pieces = 8
    whole = lambda shape: pl.BlockSpec(shape, lambda i: (0,) * len(shape))
    return pl.pallas_call(
        functools.partial(apply_kernel, math.sqrt(height * rows * cols)),
        grid=(pieces,),
        out_shape=(
            jax.ShapeDtypeStruct((height, rank), F32),
            jax.ShapeDtypeStruct((rank, width), F32),
        ),
        in_specs=[
            pl.BlockSpec((units // pieces, TILE, LANES), lambda i: (i, 0, 0)),
            whole((height, rank)),
            whole((rank, rank)),
        ],
        out_specs=(whole((height, rank)), pl.BlockSpec((rank, width // pieces), lambda i: (0, i))),
        compiler_params=pltpu.CompilerParams(vmem_limit_bytes=16 * 2**20),
    )(total, sampled, inverse)


def solution(mesh):
    rows, cols = mesh.shape["row"], mesh.shape["col"]
    placed = (P(("row", "col"), None), P())
    return jax.shard_map(
        functools.partial(per_device, rows, cols),
        mesh=mesh,
        in_specs=placed,
        out_specs=placed,
        check_vma=False,
    )
```

time: 309 us -> 98.1 us (0.32); the launches traced: 303 us -> 97.8 us
  waiting for transfers between devices: 153 us -> 0 us
  Pallas kernels: 0 us -> 93.2 us
  other arithmetic: 88.6 us -> 0 us
  matrix products: 33.8 us -> 0 us
  between operations: 14.7 us -> 0.65 us
  starting transfers between devices: 6.72 us -> 0 us
    psum x1 -> x0, waiting for transfers between devices: 145 us -> none  [per_device(): lax.psum(jnp.dot(transposed, slab, precision=highest), ('row', 'col'))]
    pallas_call x0 -> x2, Pallas kernels: none -> 93.2 us  [the longest x1 86.8 us: per_device(): pl.pallas_call(functools.partial(sum_kernel, rows, cols), out_shape=(jax....]
    another operation x20 -> x0, other arithmetic: 85.2 us -> none  [the longest x15 62.4 us: merge_level(): return jnp.linalg.cholesky(combined)]
    dot_general x13 -> x0, matrix products: 33.4 us -> none  [the longest x1 16.4 us: per_device(): jnp.dot(slab, sketch, precision=highest, preferred_element_type=jnp.float32)]
    ppermute x5 -> x0, waiting for transfers between devices: 8.41 us -> none  [from_partner(): return lax.ppermute(value, axis, pairs)]
    ppermute x5 -> x0, starting transfers between devices: 6.68 us -> none  [from_partner(): return lax.ppermute(value, axis, pairs)]
    select_n x5 -> x0, other arithmetic: 3.28 us -> none  [the longest x4 2.63 us: merge_level(): return jnp.linalg.cholesky(combined)]
  transfers between devices with their start and end apart: 6 -> 0, of which waited for: 6 -> 0; matrix products, arithmetic and copies ran while one was open for 1% -> 0% of each run, Pallas kernels for 0% -> 0%
where the time goes in v1:
time: 98.1 us; the launch traced here: 97.8 us
  Pallas kernels  93.2 us (95%)
  local copies, waits for them, and re-layouts  3.97 us (4%)
    pallas_call x1, Pallas kernels, per_device(): pl.pallas_call(functools.partial(sum_kernel, rows, cols), out_shape=(jax....  86.8 us
    pallas_call x1, Pallas kernels, per_device(): pl.pallas_call(functools.partial(apply_kernel, math.sqrt(height * rows *...  6.41 us
    unnamed x6, local copies, waits for them, and re-layouts  3.97 us

profile of v1, /device:TPU:1, one launch (start us, length us, event | category | flops | bytes accessed | tf_op | source)
XLA Modules:
  0.0 97.8 jit_solution(14455033251388790583)
XLA Ops:
  0.6 86.8 %shard_map.41 = (f32[1024,8,128]{2,1,0:T(8,128)}, f32[512,128]{1,0:T(8,128)}, f32[128,128]{1,0:T(8,128)}) custom-call(f32[512,8192]{1,0:T(8,128)} %slab.1, f32[8192,128]{1,0:T(8,128)} %sketch.1), custom_call_target="tpu_custom_call" | custom-call | tf_op jit(solution)/shard_map/pallas_call | solution.py:266
  87.4 0.0 copy-start
  87.4 2.2 %copy-done = f32[1024,8,128]{2,1,0:T(8,128)S(1)} copy-done((f32[1024,8,128]{2,1,0:T(8,128)S(1)}, f32[1024,8,128]{2,1,0:T(8,128)}, u32[]{:S(2)}) %copy-start) | copy-done | bytes 4194328
  89.6 0.0 copy-start.1
  89.6 0.9 copy-done.1
  90.6 0.0 copy-start.2
  90.6 0.8 copy-done.2
  91.4 6.4 %shard_map.42 = (f32[512,128]{1,0:T(8,128)}, f32[128,8192]{1,0:T(8,128)}) custom-call(f32[1024,8,128]{2,1,0:T(8,128)S(1)} %copy-done, f32[512,128]{1,0:T(8,128)S(1)} %copy-done.1, f32[128,128]{1,0:T(8,128)S(1)} %copy-done.2), custom_call_target="tpu_custom_call" | custom-call | tf_op jit(solution)/shard_map/pallas_call | solution.py:300
Async XLA Ops:
  87.4 2.2 %copy-start = (f32[1024,8,128]{2,1,0:T(8,128)S(1)}, f32[1024,8,128]{2,1,0:T(8,128)}, u32[]{:S(2)}) copy-start(f32[1024,8,128]{2,1,0:T(8,128)} %get-tuple-element.5.total_ref) | copy-start | bytes 12582916
  89.6 0.9 copy-start.1
  90.6 0.8 copy-start.2

commit v2 on v1

--- a/solution.py
+++ b/solution.py
@@ -15,8 +15,10 @@
 TILE = 8
 LOAD = 512
 WIDE = 256
-CHUNKS = 8
-CHOL = 16
+MOST_CHUNKS = 16
+HOP = 2
+PANEL = 32
+CHOL = 8
 
 
 def split(value):
@@ -53,15 +55,17 @@
 
 
 def sum_kernel(
-    rows, cols, slab, sketch, total_ref, sampled_ref, inverse_ref,
-    staged, sk, high, low, part, landed, left, grams, gram_in, work, wide_acc, slab_sem, sk_sem,
-    send_sem, recv_sem, gram_send, gram_recv,
+    rows, cols, slab, sketch, total_out, sampled_out, inverse_out,
+    staged, sk, high, low, part, landed, total_ref, sampled_ref, inverse_ref, left, grams, gram_in,
+    work, panel, wide_acc, slab_sem, sk_sem, send_sem, recv_sem, gram_send, gram_recv, total_sem,
+    out_sem,
 ):
     height, width = slab.shape
     bits = (rows * cols).bit_length() - 1
     units = width // LANES * (LANES // TILE)
-    chunk_units = units // CHUNKS
-    chunk_cols = width // CHUNKS
+    chunks = min(MOST_CHUNKS, units >> bits)
+    chunk_units = units // chunks
+    chunk_cols = width // chunks
     loads = width // LOAD
 
     sketch_copy = pltpu.make_async_copy(sketch, sk, sk_sem)
@@ -75,7 +79,7 @@
     for i in range(loads):
         load(i).start()
 
-    orders = [chunk_order(k, rows, cols) for k in range(CHUNKS)]
+    orders = [chunk_order(k, rows, cols) for k in range(chunks)]
     gram_order = [("row", 0)] + [b for b in orders[0][0] if b != ("row", 0)]
     barrier = pltpu.get_barrier_semaphore()
     for place in gram_order:
@@ -100,6 +104,8 @@
     lax.fori_loop(0, loads, sample, 0)
     sampled = wide_acc[:, :LANES] + wide_acc[:, LANES:]
     sampled_ref[...] = sampled
+    sampled_copy = pltpu.make_async_copy(sampled_ref, sampled_out, out_sem.at[0])
+    sampled_copy.start()
     turned = sampled.T
     t_high, t_low = split(turned)
     left[:LANES, :] = t_high
@@ -127,7 +133,7 @@
         lax.fori_loop(0, chunk_cols // WIDE, body, 0)
 
     plan = []
-    for k in range(CHUNKS):
+    for k in range(chunks):
         start, size, steps = k * chunk_units, chunk_units, []
         for even, odd in zip(*orders[k]):
             device, bit = pick(even, odd)
@@ -169,6 +175,10 @@
             device_id=device,
             device_id_type=MESH,
         )
+
+    def deliver(k):
+        region = pl.ds(k * chunk_units, chunk_units)
+        return pltpu.make_async_copy(total_ref.at[region], total_out.at[region], total_sem.at[k])
 
     def chunk_step(k, s):
         if s == 0:
@@ -188,48 +198,77 @@
             gather(k, 2 * bits - s).wait_recv()
             if s < 2 * bits:
                 gather(k, 2 * bits - s - 1).start()
+            else:
+                deliver(k).start()
 
     def gram_step(t):
-        if 1 <= t <= bits:
-            exchange_gram(t - 1).wait_recv()
-            grams[t] = grams[t - 1] + gram_in[t - 1]
-        if t < bits:
-            exchange_gram(t).start()
-        if t == bits:
-            work[:, :LANES] = grams[bits]
-            work[:, LANES:] = (
-                lax.broadcasted_iota(jnp.int32, (LANES, LANES), 0)
-                == lax.broadcasted_iota(jnp.int32, (LANES, LANES), 1)
-            ).astype(F32)
-        first = (t - bits - 1) * CHOL
+        step = t // HOP
+        if t % HOP == 0:
+            if 1 <= step <= bits:
+                exchange_gram(step - 1).wait_recv()
+                grams[step] = grams[step - 1] + gram_in[step - 1]
+            if step < bits:
+                exchange_gram(step).start()
+            if step == bits:
+                work[:, :LANES] = grams[bits]
+                work[:, LANES:] = (square_rows == square_lanes).astype(F32)
+        first = (t - HOP * bits - 1) * CHOL
         if 0 <= first < LANES:
             eliminate(first)
 
+    square_rows = lax.broadcasted_iota(jnp.int32, (LANES, LANES), 0)
+    square_lanes = lax.broadcasted_iota(jnp.int32, (LANES, LANES), 1)
+    panel_rows = lax.broadcasted_iota(jnp.int32, (PANEL, LANES), 0)
+    panel_lanes = lax.broadcasted_iota(jnp.int32, (PANEL, LANES), 1)
+
     def eliminate(first):
-        lane = lax.broadcasted_iota(jnp.int32, (LANES, LANES), 1)
-        sub = lax.broadcasted_iota(jnp.int32, (LANES, 1), 0)
-
-        def body(j, carry):
-            all_rows = work[...]
-            column = jnp.sum(jnp.where(lane == j, all_rows[:, :LANES], 0.0), axis=1, keepdims=True)
-            row = work[pl.ds(j, 1), :]
-            pivot = jnp.sum(jnp.where(sub == j, column, 0.0), axis=0, keepdims=True)
-            scale = 1.0 / jnp.sqrt(pivot)
-            row = row * scale
-            below = jnp.where(sub > j, column * scale, 0.0)
-            work[...] = jnp.where(sub == j, row, all_rows - below * row)
-            return carry
-
-        lax.fori_loop(first, first + CHOL, body, 0)
-
-    for t in range(max(CHUNKS + 2 * bits, bits + 1 + LANES // CHOL)):
+        base = first // PANEL * PANEL
+        here = pl.ds(base, PANEL)
+        if first == base:
+            block = work[here, :LANES]
+            if base:
+                block = pltpu.roll(block, LANES - base, 1)
+            unit = (panel_rows + PANEL == panel_lanes).astype(F32)
+            value = jnp.where(panel_lanes < PANEL, block, unit)
+        else:
+            value = panel[...]
+        for j in range(first - base, first - base + CHOL):
+            ratio = value[:, j : j + 1] / value[j : j + 1, j : j + 1]
+            below = jnp.where(panel_rows > j, ratio, 0.0)
+            value = value - below * value[j : j + 1, :]
+        panel[...] = value
+        if first + CHOL < base + PANEL:
+            return
+        diagonal = jnp.sum(
+            jnp.where(panel_rows == panel_lanes, value, 0.0), axis=1, keepdims=True
+        )
+        value = value / jnp.sqrt(diagonal)
+        shift = (base - PANEL) % LANES
+        if shift:
+            value = pltpu.roll(value, shift, 1)
+        inside = jnp.logical_and(panel_lanes >= base, panel_lanes < base + PANEL)
+        value = jnp.where(inside, value, 0.0)
+        highest = lax.Precision.HIGHEST
+        done = jnp.dot(value, work[...], precision=highest, preferred_element_type=F32)
+        work[here, :] = done
+        if base + PANEL < LANES:
+            change = jnp.dot(done[:, :LANES].T, done, precision=highest, preferred_element_type=F32)
+            rest = slice(base + PANEL, LANES)
+            work[rest, :] = work[rest, :] - change[rest, :]
+        else:
+            inverse_ref[...] = work[:, LANES:]
+            pltpu.make_async_copy(inverse_ref, inverse_out, out_sem.at[1]).start()
+
+    for t in range(max(chunks + HOP * 2 * bits, HOP * bits + 1 + LANES // CHOL)):
         gram_step(t)
-        for k in range(CHUNKS):
-            if 0 <= t - k <= 2 * bits:
-                chunk_step(k, t - k)
-
-    inverse_ref[...] = work[:, LANES:]
-    for k in range(CHUNKS):
+        for k in range(chunks):
+            if t >= k and (t - k) % HOP == 0 and (t - k) // HOP <= 2 * bits:
+                chunk_step(k, (t - k) // HOP)
+
+    sampled_copy.wait()
+    pltpu.make_async_copy(inverse_ref, inverse_out, out_sem.at[1]).wait()
+    for k in range(chunks):
+        deliver(k).wait()
         for s in range(bits):
             scatter(k, s).wait_send()
             gather(k, s).wait_send()
@@ -254,7 +293,13 @@
     value = jnp.concatenate(
         [total_ref[b * per : (b + 1) * per].reshape(LANES, LANES) for b in range(blocks)], axis=1
     )
-    projection_ref[...] = jnp.dot(inverse, value, precision=highest, preferred_element_type=F32)
+    v_high, v_low = split(value)
+    i_high, i_low = split(inverse)
+    projection_ref[...] = jnp.dot(
+        jnp.concatenate([i_high, i_high], axis=1),
+        jnp.concatenate([v_high, v_low], axis=0),
+        preferred_element_type=F32,
+    ) + jnp.dot(i_low, v_high, preferred_element_type=F32)
 
 
 def per_device(rows, cols, slab, sketch):
@@ -262,7 +307,8 @@
     rank = sketch.shape[1]
     bits = (rows * cols).bit_length() - 1
     units = width // LANES * (rank // TILE)
-    vmem = pl.BlockSpec(memory_space=pltpu.VMEM)
+    chunks = min(MOST_CHUNKS, units >> bits)
+    anywhere = pl.BlockSpec(memory_space=pl.ANY)
     total, sampled, inverse = pl.pallas_call(
         functools.partial(sum_kernel, rows, cols),
         out_shape=(
@@ -270,8 +316,8 @@
             jax.ShapeDtypeStruct((height, rank), F32),
             jax.ShapeDtypeStruct((rank, rank), F32),
         ),
-        in_specs=[pl.BlockSpec(memory_space=pl.ANY)] * 2,
-        out_specs=(vmem, vmem, vmem),
+        in_specs=[anywhere] * 2,
+        out_specs=(anywhere,) * 3,
         scratch_shapes=[
             pltpu.VMEM((width // LOAD, height, LOAD), F32),
             pltpu.VMEM((width, rank), F32),
@@ -279,17 +325,23 @@
             pltpu.VMEM((height, width), BF16),
             pltpu.VMEM((units, TILE, LANES), F32),
             pltpu.VMEM((units, TILE, LANES), F32),
+            pltpu.VMEM((units, TILE, LANES), F32),
+            pltpu.VMEM((height, rank), F32),
+            pltpu.VMEM((rank, rank), F32),
             pltpu.VMEM((2 * rank, height), BF16),
             pltpu.VMEM((bits + 1, rank, rank), F32),
             pltpu.VMEM((bits, rank, rank), F32),
             pltpu.VMEM((rank, 2 * rank), F32),
+            pltpu.VMEM((PANEL, rank), F32),
             pltpu.VMEM((height, 2 * rank), F32),
             pltpu.SemaphoreType.DMA((width // LOAD,)),
             pltpu.SemaphoreType.DMA,
-            pltpu.SemaphoreType.DMA((CHUNKS, 2 * bits)),
-            pltpu.SemaphoreType.DMA((CHUNKS, 2 * bits)),
+            pltpu.SemaphoreType.DMA((chunks, 2 * bits)),
+            pltpu.SemaphoreType.DMA((chunks, 2 * bits)),
             pltpu.SemaphoreType.DMA((bits,)),
             pltpu.SemaphoreType.DMA((bits,)),
+            pltpu.SemaphoreType.DMA((chunks,)),
+            pltpu.SemaphoreType.DMA((2,)),
         ],
         compiler_params=pltpu.CompilerParams(
             collective_id=0, has_side_effects=True, vmem_limit_bytes=56 * 2**20
@@ -310,7 +362,7 @@
             whole((rank, rank)),
         ],
         out_specs=(whole((height, rank)), pl.BlockSpec((rank, width // pieces), lambda i: (0, i))),
-        compiler_params=pltpu.CompilerParams(vmem_limit_bytes=16 * 2**20),
+        compiler_params=pltpu.CompilerParams(vmem_limit_bytes=56 * 2**20),
     )(total, sampled, inverse)
 
 

time: 98.1 us -> 88.3 us (0.900)
  Pallas kernels: 93.2 us -> 87.4 us
  local copies, waits for them, and re-layouts: 3.97 us -> 0 us
    pallas_call x1, Pallas kernels: 86.8 us -> 79.4 us  [per_device(): pl.pallas_call(functools.partial(sum_kernel, rows, cols), out_shape=(jax....]
    unnamed x6 -> x0, local copies, waits for them, and re-layouts: 3.97 us -> none
    pallas_call x1, Pallas kernels: 6.41 us -> 8.01 us  [per_device(): pl.pallas_call(functools.partial(apply_kernel, math.sqrt(height * rows *...]
where the time goes in v2:
time: 88.3 us; the launch traced here: 88.1 us
  Pallas kernels  87.4 us (99%)
    pallas_call x1, Pallas kernels, per_device(): pl.pallas_call(functools.partial(sum_kernel, rows, cols), out_shape=(jax....  79.4 us
    pallas_call x1, Pallas kernels, per_device(): pl.pallas_call(functools.partial(apply_kernel, math.sqrt(height * rows *...  8.01 us

profile of v2, /device:TPU:1, one launch (start us, length us, event | category | flops | bytes accessed | tf_op | source)
XLA Modules:
  0.0 88.1 jit_solution(9779795564934792874)
XLA Ops:
  0.6 79.4 %shard_map.41 = (f32[1024,8,128]{2,1,0:T(8,128)}, f32[512,128]{1,0:T(8,128)}, f32[128,128]{1,0:T(8,128)}) custom-call(f32[512,8192]{1,0:T(8,128)} %slab.1, f32[8192,128]{1,0:T(8,128)} %sketch.1), custom_call_target="tpu_custom_call" | custom-call | tf_op jit(solution)/shard_map/pallas_call | solution.py:312
  80.1 8.0 %shard_map.42 = (f32[512,128]{1,0:T(8,128)}, f32[128,8192]{1,0:T(8,128)}) custom-call(f32[1024,8,128]{2,1,0:T(8,128)} %get-tuple-element.5.total_ref, f32[512,128]{1,0:T(8,128)} %get-tuple-element.6.sampled_ref, f32[128,128]{1,0:T(8,128)} %get-tuple-element.7.inverse_ref), custom_call_target="tpu_custom_call" | custom-call | tf_op jit(solution)/shard_map/pallas_call | solution.py:352

commit v3 on v2

v3 whole, which is shorter than its diff:
```python
import functools
import math

import jax
import jax.numpy as jnp
from jax import lax
from jax.experimental import pallas as pl
from jax.experimental.pallas import tpu as pltpu
from jax.sharding import PartitionSpec as P

MESH = pl.DeviceIdType.MESH
BF16 = jnp.bfloat16
F32 = jnp.float32
LANES = 128
TILE = 8
LOAD = 512
MOST_CHUNKS = 16
HOP = 2
PANEL = 32
CHOL = 16


def split(value):
    high = value.astype(BF16)
    return high, (value - high.astype(F32)).astype(BF16)


def bit_of(axis, bit):
    index = lax.axis_index(axis)
    value = (index // 2**bit) % 2
    return {axis: 2**bit * (1 - 2 * value)}, value


def orders(rows, cols):
    row_bits = [("row", b) for b in range(1, rows.bit_length() - 1)]
    col_bits = [("col", b) for b in range(cols.bit_length() - 1)]
    inner = 1 if len(col_bits) == 3 else len(col_bits) // 2
    near, far = col_bits[:inner], col_bits[inner:]
    core = [("row", 0)]
    return (
        (core + near + far + row_bits, core + row_bits + far + near),
        (core + near + row_bits + far, core + row_bits + near + far),
    )


def pick(even, odd):
    core = lax.axis_index("row") % 2
    device = {"row": lax.axis_index("row"), "col": lax.axis_index("col")}
    bit = 0
    for (axis, place), weight in ((even, 1 - core), (odd, core)):
        step, value = bit_of(axis, place)
        device[axis] = device[axis] + weight * step[axis]
        bit = bit + weight * value
    return (device["row"], device["col"]), bit


def sum_kernel(
    rows, cols, slab, sketch, basis_out, projection_out,
    staged, sk, high, low, part, landed, total, basis, left, grams, gram_in, work, panel, wide_acc,
    slab_sem, sk_sem, send_sem, recv_sem, gram_send, gram_recv, out_sem, basis_sem,
):
    height, width = slab.shape
    bits = (rows * cols).bit_length() - 1
    units = width // LANES * (LANES // TILE)
    chunks = min(MOST_CHUNKS, units >> bits)
    chunk_units = units // chunks
    chunk_cols = width // chunks
    loads = width // LOAD

    sketch_copy = pltpu.make_async_copy(sketch, sk, sk_sem)
    sketch_copy.start()

    def load(i):
        return pltpu.make_async_copy(
            slab.at[:, pl.ds(pl.multiple_of(i * LOAD, LOAD), LOAD)], staged.at[i], slab_sem.at[i]
        )

    for i in range(loads):
        load(i).start()

    plans = orders(rows, cols)
    gram_order = plans[0][0]
    barrier = pltpu.get_barrier_semaphore()
    for place in gram_order:
        device, _ = pick(place, place)
        pl.semaphore_signal(barrier, inc=1, device_id=device, device_id_type=MESH)

    wide_acc[...] = jnp.zeros_like(wide_acc)
    sketch_copy.wait()

    def sample(i, carry):
        load(i).wait()
        a_high, a_low = split(staged[i])
        columns = pl.ds(pl.multiple_of(i * LOAD, LOAD), LOAD)
        high[:, columns] = a_high
        low[:, columns] = a_low
        s_high, s_low = split(sk[columns, :])
        both = jnp.concatenate([s_high, s_low], axis=1)
        wide_acc[...] += jnp.dot(a_high, both, preferred_element_type=F32)
        wide_acc[:, :LANES] += jnp.dot(a_low, s_high, preferred_element_type=F32)
        return carry

    lax.fori_loop(0, loads, sample, 0)
    sampled = wide_acc[:, :LANES] + wide_acc[:, LANES:]
    basis[...] = sampled
    turned = sampled.T
    t_high, t_low = split(turned)
    left[:LANES, :] = t_high
    left[LANES:, :] = t_low
    grams[0] = jnp.dot(
        turned, sampled, precision=lax.Precision.HIGHEST, preferred_element_type=F32
    )
    pl.semaphore_wait(barrier, bits)

    per = LANES // TILE
    strips = chunk_cols // LOAD

    def product(k):
        for i in range(strips):
            columns = pl.ds(pl.multiple_of((k * strips + i) * LOAD, LOAD), LOAD)
            both = jnp.dot(left[...], high[:, columns], preferred_element_type=F32)
            more = jnp.dot(left[:LANES, :], low[:, columns], preferred_element_type=F32)
            value = both[:LANES] + both[LANES:] + more
            for j in range(LOAD // LANES):
                first = k * chunk_units + (i * (LOAD // LANES) + j) * per
                part[pl.ds(first, per)] = value[:, j * LANES : (j + 1) * LANES].reshape(
                    per, TILE, LANES
                )

    tables = []
    for even, odd in plans:
        start, size, steps = 0, chunk_units, []
        for step_even, step_odd in zip(even, odd):
            device, bit = pick(step_even, step_odd)
            half = size // 2
            steps.append((*device, start + bit * half, start + (1 - bit) * half))
            start, size = start + bit * half, half
        tables.append(steps)

    def place(k, s):
        second = (k % 3) // 2
        row, col, keep, give = (
            a + second * (b - a) for a, b in zip(tables[0][s], tables[1][s])
        )
        half = chunk_units >> (s + 1)
        base = k * chunk_units
        return (row, col), base + keep, base + give, half, base + chunk_units - 2 * half

    def scatter(k, s):
        device, _, give, half, slot = place(k, s)
        return pltpu.make_async_remote_copy(
            src_ref=part.at[pl.ds(give, half)],
            dst_ref=landed.at[pl.ds(slot, half)],
            send_sem=send_sem.at[k, s],
            recv_sem=recv_sem.at[k, s],
            device_id=device,
            device_id_type=MESH,
        )

    def gather(k, s):
        device, keep, _, half, _ = place(k, s)
        return pltpu.make_async_remote_copy(
            src_ref=total.at[pl.ds(keep, half)],
            dst_ref=total.at[pl.ds(keep, half)],
            send_sem=send_sem.at[k, 2 * bits - 1 - s],
            recv_sem=recv_sem.at[k, 2 * bits - 1 - s],
            device_id=device,
            device_id_type=MESH,
        )

    def exchange_gram(s):
        device, _ = pick(gram_order[s], gram_order[s])
        return pltpu.make_async_remote_copy(
            src_ref=grams.at[s],
            dst_ref=gram_in.at[s],
            send_sem=gram_send.at[s],
            recv_sem=gram_recv.at[s],
            device_id=device,
            device_id_type=MESH,
        )

    def deliver(strip):
        return pltpu.make_async_copy(
            staged.at[strip, pl.ds(0, LANES)],
            projection_out.at[:, pl.ds(pl.multiple_of(strip * LOAD, LOAD), LOAD)],
            out_sem.at[strip],
        )

    def apply(k):
        inverse = work[:, LANES:]
        i_high, i_low = split(inverse)
        doubled = jnp.concatenate([i_high, i_high], axis=1)
        for i in range(strips):
            first = k * chunk_units + i * (LOAD // LANES) * per
            value = jnp.concatenate(
                [
                    total[pl.ds(first + j * per, per)].reshape(LANES, LANES)
                    for j in range(LOAD // LANES)
                ],
                axis=1,
            )
            v_high, v_low = split(value)
            strip = k * strips + i
            staged[strip, :LANES, :] = jnp.dot(
                doubled, jnp.concatenate([v_high, v_low], axis=0), preferred_element_type=F32
            ) + jnp.dot(i_low, v_high, preferred_element_type=F32)
            deliver(strip).start()

    def chunk_step(k, s):
        if s == 0:
            product(k)
            scatter(k, 0).start()
        elif s <= bits:
            scatter(k, s - 1).wait_recv()
            _, keep, _, half, slot = place(k, s - 1)
            value = part[pl.ds(keep, half)] + landed[pl.ds(slot, half)]
            if s < bits:
                part[pl.ds(keep, half)] = value
                scatter(k, s).start()
            else:
                total[pl.ds(keep, half)] = value
                gather(k, bits - 1).start()
        else:
            gather(k, 2 * bits - s).wait_recv()
            if s < 2 * bits:
                gather(k, 2 * bits - s - 1).start()
            else:
                apply(k)

    square_rows = lax.broadcasted_iota(jnp.int32, (LANES, LANES), 0)
    square_lanes = lax.broadcasted_iota(jnp.int32, (LANES, LANES), 1)
    panel_rows = lax.broadcasted_iota(jnp.int32, (PANEL, LANES), 0)
    panel_lanes = lax.broadcasted_iota(jnp.int32, (PANEL, LANES), 1)
    highest = lax.Precision.HIGHEST
    basis_copy = pltpu.make_async_copy(basis, basis_out, basis_sem)

    def gram_step(step):
        if step >= 1:
            exchange_gram(step - 1).wait_recv()
            grams[step] = grams[step - 1] + gram_in[step - 1]
        if step < bits:
            exchange_gram(step).start()
        else:
            work[:, :LANES] = grams[bits]
            work[:, LANES:] = (square_rows == square_lanes).astype(F32)

    def eliminate(base, piece):
        here = pl.ds(pl.multiple_of(base, PANEL), PANEL)
        if piece == 0:
            block = pltpu.roll(work[here, :LANES], (LANES - base) % LANES, 1)
            unit = (panel_rows + PANEL == panel_lanes).astype(F32)
            value = jnp.where(panel_lanes < PANEL, block, unit)
        else:
            value = panel[...]
        for j in range(piece * CHOL, (piece + 1) * CHOL):
            column = jnp.broadcast_to(value[:, j : j + 1], (PANEL, LANES))
            row = value[j : j + 1, :] / column[j : j + 1, :]
            value = value - jnp.where(panel_rows > j, column, 0.0) * row
        panel[...] = value
        if (piece + 1) * CHOL < PANEL:
            return
        diagonal = jnp.sum(
            jnp.where(panel_rows == panel_lanes, value, 0.0), axis=1, keepdims=True
        )
        value = pltpu.roll(value / jnp.sqrt(diagonal), (base + LANES - PANEL) % LANES, 1)
        inside = jnp.logical_and(panel_lanes >= base, panel_lanes < base + PANEL)
        value = jnp.where(inside, value, 0.0)
        done = jnp.dot(value, work[...], precision=highest, preferred_element_type=F32)
        work[here, :] = done
        change = jnp.dot(done[:, :LANES].T, done, precision=highest, preferred_element_type=F32)
        rest = lax.broadcasted_iota(jnp.int32, (LANES, 2 * LANES), 0) >= base + PANEL
        work[...] = jnp.where(rest, work[...] - change, work[...])

    def make_basis():
        product_turned = lax.dot_general(
            basis[...], work[:, LANES:], (((1,), (1,)), ((), ())),
            precision=highest, preferred_element_type=F32,
        )
        basis[...] = product_turned * math.sqrt(height * rows * cols)
        basis_copy.start()

    first_elimination = HOP * bits + 1
    pieces = PANEL // CHOL

    def tick(t, carry):
        for step in range(bits + 1):
            pl.when(t == HOP * step)(functools.partial(gram_step, step))
        for s in reversed(range(2 * bits + 1)):
            k = t - HOP * s
            pl.when(jnp.logical_and(k >= 0, k < chunks))(functools.partial(chunk_step, k, s))
        done = t - first_elimination
        for piece in range(pieces):
            due = jnp.logical_and(done >= 0, done < LANES // CHOL)
            base = done // pieces * PANEL
            pl.when(jnp.logical_and(due, done % pieces == piece))(
                functools.partial(eliminate, base, piece)
            )
        pl.when(done == LANES // CHOL)(make_basis)
        return carry

    lax.fori_loop(0, chunks + HOP * 2 * bits, tick, 0)

    def drain(k, carry):
        for s in range(bits):
            scatter(k, s).wait_send()
            gather(k, s).wait_send()
        for i in range(strips):
            deliver(k * strips + i).wait()
        return carry

    lax.fori_loop(0, chunks, drain, 0)
    basis_copy.wait()
    for s in range(bits):
        exchange_gram(s).wait_send()


def per_device(rows, cols, slab, sketch):
    height, width = slab.shape
    rank = sketch.shape[1]
    bits = (rows * cols).bit_length() - 1
    units = width // LANES * (rank // TILE)
    chunks = min(MOST_CHUNKS, units >> bits)
    anywhere = pl.BlockSpec(memory_space=pl.ANY)
    return pl.pallas_call(
        functools.partial(sum_kernel, rows, cols),
        out_shape=(
            jax.ShapeDtypeStruct((height, rank), F32),
            jax.ShapeDtypeStruct((rank, width), F32),
        ),
        in_specs=[anywhere] * 2,
        out_specs=(anywhere,) * 2,
        scratch_shapes=[
            pltpu.VMEM((width // LOAD, height, LOAD), F32),
            pltpu.VMEM((width, rank), F32),
            pltpu.VMEM((height, width), BF16),
            pltpu.VMEM((height, width), BF16),
            pltpu.VMEM((units, TILE, LANES), F32),
            pltpu.VMEM((units, TILE, LANES), F32),
            pltpu.VMEM((units, TILE, LANES), F32),
            pltpu.VMEM((height, rank), F32),
            pltpu.VMEM((2 * rank, height), BF16),
            pltpu.VMEM((bits + 1, rank, rank), F32),
            pltpu.VMEM((bits, rank, rank), F32),
            pltpu.VMEM((rank, 2 * rank), F32),
            pltpu.VMEM((PANEL, rank), F32),
            pltpu.VMEM((height, 2 * rank), F32),
            pltpu.SemaphoreType.DMA((width // LOAD,)),
            pltpu.SemaphoreType.DMA,
            pltpu.SemaphoreType.DMA((chunks, 2 * bits)),
            pltpu.SemaphoreType.DMA((chunks, 2 * bits)),
            pltpu.SemaphoreType.DMA((bits,)),
            pltpu.SemaphoreType.DMA((bits,)),
            pltpu.SemaphoreType.DMA((width // LOAD,)),
            pltpu.SemaphoreType.DMA,
        ],
        compiler_params=pltpu.CompilerParams(
            collective_id=0, has_side_effects=True, vmem_limit_bytes=56 * 2**20
        ),
    )(slab, sketch)


def solution(mesh):
    rows, cols = mesh.shape["row"], mesh.shape["col"]
    placed = (P(("row", "col"), None), P())
    return jax.shard_map(
        functools.partial(per_device, rows, cols),
        mesh=mesh,
        in_specs=placed,
        out_specs=placed,
        check_vma=False,
    )
```

time: 88.3 us -> 89.8 us (1.017)
  local copies, waits for them, and re-layouts: 0 us -> 6.27 us
  Pallas kernels: 87.4 us -> 82.7 us
    pallas_call x1 -> x0, Pallas kernels: 8.01 us -> none  [per_device(): pl.pallas_call(functools.partial(apply_kernel, math.sqrt(height * rows *...]
    unnamed x0 -> x2, local copies, waits for them, and re-layouts: none -> 6.27 us
    pallas_call x1, Pallas kernels: 79.4 us -> 82.7 us  [per_device(): pl.pallas_call(functools.partial(sum_kernel, rows, cols), out_shape=(jax....]
where the time goes in v3:
time: 89.8 us; the launch traced here: 89.6 us
  Pallas kernels  82.7 us (92%)
  local copies, waits for them, and re-layouts  6.27 us (7%)
    pallas_call x1, Pallas kernels, per_device(): pl.pallas_call(functools.partial(sum_kernel, rows, cols), out_shape=(jax....  82.7 us
    unnamed x2, local copies, waits for them, and re-layouts  6.27 us

profile of v3, /device:TPU:1, one launch (start us, length us, event | category | flops | bytes accessed | tf_op | source)
XLA Modules:
  0.0 89.6 jit_solution(13053226982560837831)
XLA Ops:
  0.6 82.7 %shard_map.41 = (f32[512,128]{1,0:T(8,128)}, f32[128,8192]{1,0:T(8,128)}) custom-call(f32[512,8192]{1,0:T(8,128)} %slab.1, f32[8192,128]{1,0:T(8,128)} %sketch.1), custom_call_target="tpu_custom_call" | custom-call | tf_op jit(solution)/shard_map/pallas_call | solution.py:324
  83.3 1.7 %copy.6 = f32[512,128]{1,0:T(8,128)} copy(f32[512,128]{1,0:T(8,128)} %get-tuple-element.4) | data formatting | bytes 524288
  85.0 4.6 %copy.7 = f32[128,8192]{1,0:T(8,128)} copy(f32[128,8192]{1,0:T(8,128)} %get-tuple-element.5) | data formatting | bytes 8388608

commit v4 on v3

--- a/solution.py
+++ b/solution.py
@@ -13,8 +13,9 @@
 F32 = jnp.float32
 LANES = 128
 TILE = 8
-LOAD = 512
-MOST_CHUNKS = 16
+LOAD = 1024
+CHUNKS = 8
+STRIP = 512
 HOP = 2
 PANEL = 32
 CHOL = 16
@@ -37,10 +38,7 @@
     inner = 1 if len(col_bits) == 3 else len(col_bits) // 2
     near, far = col_bits[:inner], col_bits[inner:]
     core = [("row", 0)]
-    return (
-        (core + near + far + row_bits, core + row_bits + far + near),
-        (core + near + row_bits + far, core + row_bits + near + far),
-    )
+    return list(zip(core + near + row_bits, core + row_bits + near)), [(b, b) for b in far]
 
 
 def pick(even, odd):
@@ -56,13 +54,13 @@
 
 def sum_kernel(
     rows, cols, slab, sketch, basis_out, projection_out,
-    staged, sk, high, low, part, landed, total, basis, left, grams, gram_in, work, panel, wide_acc,
+    staged, sk, high, low, part, landed, total, swap_in, swap_out, basis, left, grams, gram_in, work, panel, wide_acc,
     slab_sem, sk_sem, send_sem, recv_sem, gram_send, gram_recv, out_sem, basis_sem,
 ):
     height, width = slab.shape
     bits = (rows * cols).bit_length() - 1
     units = width // LANES * (LANES // TILE)
-    chunks = min(MOST_CHUNKS, units >> bits)
+    chunks = CHUNKS
     chunk_units = units // chunks
     chunk_cols = width // chunks
     loads = width // LOAD
@@ -78,11 +76,13 @@
     for i in range(loads):
         load(i).start()
 
-    plans = orders(rows, cols)
-    gram_order = plans[0][0]
+    halving, swapping = orders(rows, cols)
+    halves, swaps = len(halving), len(swapping)
+    kept_units = chunk_units >> halves
+    gram_order = [(even, even) for even, _ in halving + swapping]
     barrier = pltpu.get_barrier_semaphore()
     for place in gram_order:
-        device, _ = pick(place, place)
+        device, _ = pick(*place)
         pl.semaphore_signal(barrier, inc=1, device_id=device, device_id_type=MESH)
 
     wide_acc[...] = jnp.zeros_like(wide_acc)
@@ -113,38 +113,46 @@
     pl.semaphore_wait(barrier, bits)
 
     per = LANES // TILE
-    strips = chunk_cols // LOAD
+    strips = chunk_cols // STRIP
 
     def product(k):
         for i in range(strips):
-            columns = pl.ds(pl.multiple_of((k * strips + i) * LOAD, LOAD), LOAD)
+            columns = pl.ds(pl.multiple_of((k * strips + i) * STRIP, STRIP), STRIP)
             both = jnp.dot(left[...], high[:, columns], preferred_element_type=F32)
             more = jnp.dot(left[:LANES, :], low[:, columns], preferred_element_type=F32)
             value = both[:LANES] + both[LANES:] + more
-            for j in range(LOAD // LANES):
-                first = k * chunk_units + (i * (LOAD // LANES) + j) * per
+            for j in range(STRIP // LANES):
+                first = k * chunk_units + (i * (STRIP // LANES) + j) * per
                 part[pl.ds(first, per)] = value[:, j * LANES : (j + 1) * LANES].reshape(
                     per, TILE, LANES
                 )
 
-    tables = []
-    for even, odd in plans:
-        start, size, steps = 0, chunk_units, []
-        for step_even, step_odd in zip(even, odd):
-            device, bit = pick(step_even, step_odd)
-            half = size // 2
-            steps.append((*device, start + bit * half, start + (1 - bit) * half))
-            start, size = start + bit * half, half
-        tables.append(steps)
+    table, start = [], 0
+    for s, places in enumerate(halving):
+        device, bit = pick(*places)
+        half = chunk_units >> (s + 1)
+        table.append((device, start + bit * half, start + (1 - bit) * half))
+        start = start + bit * half
 
     def place(k, s):
-        second = (k % 3) // 2
-        row, col, keep, give = (
-            a + second * (b - a) for a, b in zip(tables[0][s], tables[1][s])
-        )
+        device, keep, give = table[s]
         half = chunk_units >> (s + 1)
         base = k * chunk_units
-        return (row, col), base + keep, base + give, half, base + chunk_units - 2 * half
+        return device, base + keep, base + give, half, base + chunk_units - 2 * half
+
+    def swap(k, s):
+        if s == 0:
+            source = part.at[pl.ds(place(k, halves - 1)[1], kept_units)]
+        else:
+            source = swap_out.at[k, s - 1]
+        return pltpu.make_async_remote_copy(
+            src_ref=source,
+            dst_ref=swap_in.at[k, s],
+            send_sem=send_sem.at[k, halves + s],
+            recv_sem=recv_sem.at[k, halves + s],
+            device_id=pick(*swapping[s])[0],
+            device_id_type=MESH,
+        )
 
     def scatter(k, s):
         device, _, give, half, slot = place(k, s)
@@ -162,14 +170,14 @@
         return pltpu.make_async_remote_copy(
             src_ref=total.at[pl.ds(keep, half)],
             dst_ref=total.at[pl.ds(keep, half)],
-            send_sem=send_sem.at[k, 2 * bits - 1 - s],
-            recv_sem=recv_sem.at[k, 2 * bits - 1 - s],
+            send_sem=send_sem.at[k, 2 * halves + swaps - 1 - s],
+            recv_sem=recv_sem.at[k, 2 * halves + swaps - 1 - s],
             device_id=device,
             device_id_type=MESH,
         )
 
     def exchange_gram(s):
-        device, _ = pick(gram_order[s], gram_order[s])
+        device, _ = pick(*gram_order[s])
         return pltpu.make_async_remote_copy(
             src_ref=grams.at[s],
             dst_ref=gram_in.at[s],
@@ -179,11 +187,11 @@
             device_id_type=MESH,
         )
 
-    def deliver(strip):
+    def deliver(k):
         return pltpu.make_async_copy(
-            staged.at[strip, pl.ds(0, LANES)],
-            projection_out.at[:, pl.ds(pl.multiple_of(strip * LOAD, LOAD), LOAD)],
-            out_sem.at[strip],
+            staged.at[k, pl.ds(0, LANES)],
+            projection_out.at[:, pl.ds(pl.multiple_of(k * chunk_cols, chunk_cols), chunk_cols)],
+            out_sem.at[k],
         )
 
     def apply(k):
@@ -191,39 +199,50 @@
         i_high, i_low = split(inverse)
         doubled = jnp.concatenate([i_high, i_high], axis=1)
         for i in range(strips):
-            first = k * chunk_units + i * (LOAD // LANES) * per
+            first = k * chunk_units + i * (STRIP // LANES) * per
             value = jnp.concatenate(
                 [
                     total[pl.ds(first + j * per, per)].reshape(LANES, LANES)
-                    for j in range(LOAD // LANES)
+                    for j in range(STRIP // LANES)
                 ],
                 axis=1,
             )
             v_high, v_low = split(value)
-            strip = k * strips + i
-            staged[strip, :LANES, :] = jnp.dot(
+            staged[k, :LANES, i * STRIP : (i + 1) * STRIP] = jnp.dot(
                 doubled, jnp.concatenate([v_high, v_low], axis=0), preferred_element_type=F32
             ) + jnp.dot(i_low, v_high, preferred_element_type=F32)
-            deliver(strip).start()
+        deliver(k).start()
+
+    last = 2 * halves + swaps
 
     def chunk_step(k, s):
         if s == 0:
             product(k)
             scatter(k, 0).start()
-        elif s <= bits:
+        elif s <= halves:
             scatter(k, s - 1).wait_recv()
             _, keep, _, half, slot = place(k, s - 1)
-            value = part[pl.ds(keep, half)] + landed[pl.ds(slot, half)]
-            if s < bits:
-                part[pl.ds(keep, half)] = value
+            part[pl.ds(keep, half)] = part[pl.ds(keep, half)] + landed[pl.ds(slot, half)]
+            if s < halves:
                 scatter(k, s).start()
             else:
-                total[pl.ds(keep, half)] = value
-                gather(k, bits - 1).start()
+                swap(k, 0).start()
+        elif s <= halves + swaps:
+            i = s - halves - 1
+            swap(k, i).wait_recv()
+            keep = place(k, halves - 1)[1]
+            mine = part[pl.ds(keep, kept_units)] if i == 0 else swap_out[k, i - 1]
+            value = mine + swap_in[k, i]
+            if i + 1 < swaps:
+                swap_out[k, i] = value
+                swap(k, i + 1).start()
+            else:
+                total[pl.ds(keep, kept_units)] = value
+                gather(k, halves - 1).start()
         else:
-            gather(k, 2 * bits - s).wait_recv()
-            if s < 2 * bits:
-                gather(k, 2 * bits - s - 1).start()
+            gather(k, last - s).wait_recv()
+            if s < last:
+                gather(k, last - s - 1).start()
             else:
                 apply(k)
 
@@ -252,10 +271,18 @@
             value = jnp.where(panel_lanes < PANEL, block, unit)
         else:
             value = panel[...]
-        for j in range(piece * CHOL, (piece + 1) * CHOL):
-            column = jnp.broadcast_to(value[:, j : j + 1], (PANEL, LANES))
-            row = value[j : j + 1, :] / column[j : j + 1, :]
-            value = value - jnp.where(panel_rows > j, column, 0.0) * row
+        for j in range(piece * CHOL, (piece + 1) * CHOL, 2):
+            first = jnp.broadcast_to(value[:, j : j + 1], (PANEL, LANES))
+            second = jnp.broadcast_to(value[:, j + 1 : j + 2], (PANEL, LANES))
+            ratio = first[j + 1 : j + 2, :] / first[j : j + 1, :]
+            top = value[j : j + 1, :]
+            next_row = value[j + 1 : j + 2, :] - ratio * top
+            pivot = second[j + 1 : j + 2, :] - ratio * first[j + 1 : j + 2, :]
+            change = first * (top / first[j : j + 1, :]) + (second - first * ratio) * (
+                next_row / pivot
+            )
+            value = jnp.where(panel_rows > j + 1, value - change, value)
+            value = jnp.where(panel_rows == j + 1, next_row, value)
         panel[...] = value
         if (piece + 1) * CHOL < PANEL:
             return
@@ -279,13 +306,13 @@
         basis[...] = product_turned * math.sqrt(height * rows * cols)
         basis_copy.start()
 
-    first_elimination = HOP * bits + 1
+    first_elimination = bits + 1
     pieces = PANEL // CHOL
 
     def tick(t, carry):
         for step in range(bits + 1):
-            pl.when(t == HOP * step)(functools.partial(gram_step, step))
-        for s in reversed(range(2 * bits + 1)):
+            pl.when(t == step)(functools.partial(gram_step, step))
+        for s in reversed(range(last + 1)):
             k = t - HOP * s
             pl.when(jnp.logical_and(k >= 0, k < chunks))(functools.partial(chunk_step, k, s))
         done = t - first_elimination
@@ -298,20 +325,34 @@
         pl.when(done == LANES // CHOL)(make_basis)
         return carry
 
-    lax.fori_loop(0, chunks + HOP * 2 * bits, tick, 0)
+    lax.fori_loop(0, chunks + HOP * last, tick, 0)
 
     def drain(k, carry):
-        for s in range(bits):
+        for s in range(halves):
             scatter(k, s).wait_send()
             gather(k, s).wait_send()
-        for i in range(strips):
-            deliver(k * strips + i).wait()
+        for s in range(swaps):
+            swap(k, s).wait_send()
+        deliver(k).wait()
         return carry
 
     lax.fori_loop(0, chunks, drain, 0)
     basis_copy.wait()
     for s in range(bits):
         exchange_gram(s).wait_send()
+
+
+def hand_over(basis, projection, basis_out, projection_out, sems):
+    copies = [pltpu.make_async_copy(basis, basis_out, sems.at[projection.shape[0] // TILE])]
+    for i in range(projection.shape[0] // TILE):
+        band = pl.ds(i * TILE, TILE)
+        copies.append(
+            pltpu.make_async_copy(projection.at[band], projection_out.at[band], sems.at[i])
+        )
+    for copy in copies:
+        copy.start()
+    for copy in copies:
+        copy.wait()
 
 
 def per_device(rows, cols, slab, sketch):
@@ -319,9 +360,10 @@
     rank = sketch.shape[1]
     bits = (rows * cols).bit_length() - 1
     units = width // LANES * (rank // TILE)
-    chunks = min(MOST_CHUNKS, units >> bits)
+    halves, swaps = (len(part) for part in orders(rows, cols))
+    kept = (units // CHUNKS) >> halves
     anywhere = pl.BlockSpec(memory_space=pl.ANY)
-    return pl.pallas_call(
+    basis, projection = pl.pallas_call(
         functools.partial(sum_kernel, rows, cols),
         out_shape=(
             jax.ShapeDtypeStruct((height, rank), F32),
@@ -337,6 +379,8 @@
             pltpu.VMEM((units, TILE, LANES), F32),
             pltpu.VMEM((units, TILE, LANES), F32),
             pltpu.VMEM((units, TILE, LANES), F32),
+            pltpu.VMEM((CHUNKS, swaps, kept, TILE, LANES), F32),
+            pltpu.VMEM((CHUNKS, swaps, kept, TILE, LANES), F32),
             pltpu.VMEM((height, rank), F32),
             pltpu.VMEM((2 * rank, height), BF16),
             pltpu.VMEM((bits + 1, rank, rank), F32),
@@ -346,17 +390,28 @@
             pltpu.VMEM((height, 2 * rank), F32),
             pltpu.SemaphoreType.DMA((width // LOAD,)),
             pltpu.SemaphoreType.DMA,
-            pltpu.SemaphoreType.DMA((chunks, 2 * bits)),
-            pltpu.SemaphoreType.DMA((chunks, 2 * bits)),
+            pltpu.SemaphoreType.DMA((CHUNKS, 2 * halves + swaps)),
+            pltpu.SemaphoreType.DMA((CHUNKS, 2 * halves + swaps)),
             pltpu.SemaphoreType.DMA((bits,)),
             pltpu.SemaphoreType.DMA((bits,)),
-            pltpu.SemaphoreType.DMA((width // LOAD,)),
+            pltpu.SemaphoreType.DMA((CHUNKS,)),
             pltpu.SemaphoreType.DMA,
         ],
         compiler_params=pltpu.CompilerParams(
             collective_id=0, has_side_effects=True, vmem_limit_bytes=56 * 2**20
         ),
     )(slab, sketch)
+    return pl.pallas_call(
+        hand_over,
+        out_shape=(
+            jax.ShapeDtypeStruct((height, rank), F32),
+            jax.ShapeDtypeStruct((rank, width), F32),
+        ),
+        in_specs=[anywhere] * 2,
+        out_specs=(anywhere,) * 2,
+        scratch_shapes=[pltpu.SemaphoreType.DMA((rank // TILE + 1,))],
+        compiler_params=pltpu.CompilerParams(vmem_limit_bytes=56 * 2**20),
+    )(basis, projection)
 
 
 def solution(mesh):

time: 89.8 us -> 210 us (2.34)
  Pallas kernels: 82.7 us -> 209 us
  local copies, waits for them, and re-layouts: 6.27 us -> 0 us
    pallas_call x0 -> x1, Pallas kernels: none -> 136 us  [per_device(): pl.pallas_call(hand_over, out_shape=(jax.ShapeDtypeStruct((height, rank),...]
    pallas_call x1, Pallas kernels: 82.7 us -> 73.1 us  [per_device(): pl.pallas_call(functools.partial(sum_kernel, rows, cols), out_shape=(jax....]
    unnamed x2 -> x0, local copies, waits for them, and re-layouts: 6.27 us -> none
where the time goes in v4:
time: 210 us
  Pallas kernels  209 us (100%)
    pallas_call x1, Pallas kernels, per_device(): pl.pallas_call(hand_over, out_shape=(jax.ShapeDtypeStruct((height, rank),...  136 us
    pallas_call x1, Pallas kernels, per_device(): pl.pallas_call(functools.partial(sum_kernel, rows, cols), out_shape=(jax....  73.1 us

profile of v4, /device:TPU:1, one launch (start us, length us, event | category | flops | bytes accessed | tf_op | source)
XLA Modules:
  0.0 210.0 jit_solution(17660179473729895353)
XLA Ops:
  0.6 73.1 %shard_map.41 = (f32[512,128]{1,0:T(8,128)}, f32[128,8192]{1,0:T(8,128)}) custom-call(f32[512,8192]{1,0:T(8,128)} %slab.1, f32[8192,128]{1,0:T(8,128)} %sketch.1), custom_call_target="tpu_custom_call" | custom-call | tf_op jit(solution)/shard_map/pallas_call | solution.py:366
  73.7 136.3 %shard_map.42 = (f32[512,128]{1,0:T(8,128)}, f32[128,8192]{1,0:T(8,128)}) custom-call(f32[512,128]{1,0:T(8,128)} %get-tuple-element.4.basis, f32[128,8192]{1,0:T(8,128)} %get-tuple-element.5.projection), custom_call_target="tpu_custom_call" | custom-call | tf_op jit(solution)/shard_map/pallas_call | solution.py:404

commit v5 on v4

--- a/solution.py
+++ b/solution.py
@@ -38,7 +38,8 @@
     inner = 1 if len(col_bits) == 3 else len(col_bits) // 2
     near, far = col_bits[:inner], col_bits[inner:]
     core = [("row", 0)]
-    return list(zip(core + near + row_bits, core + row_bits + near)), [(b, b) for b in far]
+    even, odd = core + near + far[:1] + row_bits, core + row_bits + far[:1] + near
+    return list(zip(even, odd)), [(b, b) for b in far[1:]]
 
 
 def pick(even, odd):
@@ -342,17 +343,19 @@
         exchange_gram(s).wait_send()
 
 
-def hand_over(basis, projection, basis_out, projection_out, sems):
-    copies = [pltpu.make_async_copy(basis, basis_out, sems.at[projection.shape[0] // TILE])]
-    for i in range(projection.shape[0] // TILE):
-        band = pl.ds(i * TILE, TILE)
-        copies.append(
-            pltpu.make_async_copy(projection.at[band], projection_out.at[band], sems.at[i])
-        )
-    for copy in copies:
-        copy.start()
-    for copy in copies:
-        copy.wait()
+def hand_over(basis, projection, basis_out, projection_out, basis_held, held, reads, writes):
+    pieces, height, _ = held.shape
+    moves = [(basis, basis_held, basis_out)]
+    for i in range(pieces):
+        band = pl.ds(i * height, height)
+        moves.append((projection.at[band], held.at[i], projection_out.at[band]))
+    for i, (source, middle, _) in enumerate(moves):
+        pltpu.make_async_copy(source, middle, reads.at[i]).start()
+    for i, (source, middle, target) in enumerate(moves):
+        pltpu.make_async_copy(source, middle, reads.at[i]).wait()
+        pltpu.make_async_copy(middle, target, writes.at[i]).start()
+    for i, (_, middle, target) in enumerate(moves):
+        pltpu.make_async_copy(middle, target, writes.at[i]).wait()
 
 
 def per_device(rows, cols, slab, sketch):
@@ -409,7 +412,12 @@
         ),
         in_specs=[anywhere] * 2,
         out_specs=(anywhere,) * 2,
-        scratch_shapes=[pltpu.SemaphoreType.DMA((rank // TILE + 1,))],
+        scratch_shapes=[
+            pltpu.VMEM((height, rank), F32),
+            pltpu.VMEM((rank // TILE, TILE, width), F32),
+            pltpu.SemaphoreType.DMA((rank // TILE + 1,)),
+            pltpu.SemaphoreType.DMA((rank // TILE + 1,)),
+        ],
         compiler_params=pltpu.CompilerParams(vmem_limit_bytes=56 * 2**20),
     )(basis, projection)
 

time: 210 us -> 78.8 us (0.38)
  Pallas kernels: 209 us -> 78 us
    pallas_call x1, Pallas kernels: 136 us -> 4.14 us  [per_device(): pl.pallas_call(hand_over, out_shape=(jax.ShapeDtypeStruct((height, rank),...]
where the time goes in v5:
time: 78.8 us; the launch traced here: 78.6 us
  Pallas kernels  78 us (99%)
    pallas_call x1, Pallas kernels, per_device(): pl.pallas_call(functools.partial(sum_kernel, rows, cols), out_shape=(jax....  73.9 us
    pallas_call x1, Pallas kernels, per_device(): pl.pallas_call(hand_over, out_shape=(jax.ShapeDtypeStruct((height, rank),...  4.14 us

profile of v5, /device:TPU:1, one launch (start us, length us, event | category | flops | bytes accessed | tf_op | source)
XLA Modules:
  0.0 78.6 jit_solution(17028972432983149304)
XLA Ops:
  0.6 73.9 %shard_map.41 = (f32[512,128]{1,0:T(8,128)}, f32[128,8192]{1,0:T(8,128)}) custom-call(f32[512,8192]{1,0:T(8,128)} %slab.1, f32[8192,128]{1,0:T(8,128)} %sketch.1), custom_call_target="tpu_custom_call" | custom-call | tf_op jit(solution)/shard_map/pallas_call | solution.py:369
  74.5 4.1 %shard_map.42 = (f32[512,128]{1,0:T(8,128)}, f32[128,8192]{1,0:T(8,128)}) custom-call(f32[512,128]{1,0:T(8,128)} %get-tuple-element.4.basis, f32[128,8192]{1,0:T(8,128)} %get-tuple-element.5.projection), custom_call_target="tpu_custom_call" | custom-call | tf_op jit(solution)/shard_map/pallas_call | solution.py:407

commit v6 on v5

--- a/solution.py
+++ b/solution.py
@@ -16,9 +16,10 @@
 LOAD = 1024
 CHUNKS = 8
 STRIP = 512
-HOP = 2
+SPACING = 2
+GRAM_HOP = 2
 PANEL = 32
-CHOL = 16
+CHOL = 8
 
 
 def split(value):
@@ -244,8 +245,6 @@
             gather(k, last - s).wait_recv()
             if s < last:
                 gather(k, last - s - 1).start()
-            else:
-                apply(k)
 
     square_rows = lax.broadcasted_iota(jnp.int32, (LANES, LANES), 0)
     square_lanes = lax.broadcasted_iota(jnp.int32, (LANES, LANES), 1)
@@ -307,26 +306,42 @@
         basis[...] = product_turned * math.sqrt(height * rows * cols)
         basis_copy.start()
 
-    first_elimination = bits + 1
+    first_elimination = GRAM_HOP * bits + 1
+    eliminations = LANES // CHOL
+    hops = [2 if s == 0 or s > 2 else 3 for s in range(halves)]
+    due_at = [0]
+    for hop in hops + [3] * swaps + hops[::-1]:
+        due_at.append(due_at[-1] + hop)
+    apply_at = [
+        max(due_at[-1] + SPACING * k, first_elimination + eliminations + 1 + k)
+        for k in range(chunks)
+    ]
     pieces = PANEL // CHOL
 
     def tick(t, carry):
         for step in range(bits + 1):
-            pl.when(t == step)(functools.partial(gram_step, step))
+            pl.when(t == GRAM_HOP * step)(functools.partial(gram_step, step))
         for s in reversed(range(last + 1)):
-            k = t - HOP * s
-            pl.when(jnp.logical_and(k >= 0, k < chunks))(functools.partial(chunk_step, k, s))
+            since = t - due_at[s]
+            due = jnp.logical_and(since >= 0, since < SPACING * chunks)
+            due = jnp.logical_and(due, since % SPACING == 0)
+            pl.when(due)(functools.partial(chunk_step, since // SPACING, s))
         done = t - first_elimination
         for piece in range(pieces):
-            due = jnp.logical_and(done >= 0, done < LANES // CHOL)
+            due = jnp.logical_and(done >= 0, done < eliminations)
             base = done // pieces * PANEL
             pl.when(jnp.logical_and(due, done % pieces == piece))(
                 functools.partial(eliminate, base, piece)
             )
-        pl.when(done == LANES // CHOL)(make_basis)
+        pl.when(done == eliminations)(make_basis)
+        ready, finished = 0, 0
+        for k, time in enumerate(apply_at):
+            now = jnp.where(t == time, 1, 0)
+            ready, finished = ready + now, finished + now * k
+        pl.when(ready > 0)(functools.partial(apply, finished))
         return carry
 
-    lax.fori_loop(0, chunks + HOP * last, tick, 0)
+    lax.fori_loop(0, apply_at[-1] + 1, tick, 0)
 
     def drain(k, carry):
         for s in range(halves):

time: 78.8 us -> 78.6 us (level)
  no operation moved by 1% of the time
where the time goes in v6:
time: 78.6 us; the launch traced here: 78.5 us
  Pallas kernels  77.8 us (99%)
    pallas_call x1, Pallas kernels, per_device(): pl.pallas_call(functools.partial(sum_kernel, rows, cols), out_shape=(jax....  73.7 us
    pallas_call x1, Pallas kernels, per_device(): pl.pallas_call(hand_over, out_shape=(jax.ShapeDtypeStruct((height, rank),...  4.14 us

profile of v6, /device:TPU:1, one launch (start us, length us, event | category | flops | bytes accessed | tf_op | source)
XLA Modules:
  0.0 78.5 jit_solution(17617512965280266770)
XLA Ops:
  0.6 73.7 %shard_map.41 = (f32[512,128]{1,0:T(8,128)}, f32[128,8192]{1,0:T(8,128)}) custom-call(f32[512,8192]{1,0:T(8,128)} %slab.1, f32[8192,128]{1,0:T(8,128)} %sketch.1), custom_call_target="tpu_custom_call" | custom-call | tf_op jit(solution)/shard_map/pallas_call | solution.py:384
  74.3 4.1 %shard_map.42 = (f32[512,128]{1,0:T(8,128)}, f32[128,8192]{1,0:T(8,128)}) custom-call(f32[512,128]{1,0:T(8,128)} %get-tuple-element.4.basis, f32[128,8192]{1,0:T(8,128)} %get-tuple-element.5.projection), custom_call_target="tpu_custom_call" | custom-call | tf_op jit(solution)/shard_map/pallas_call | solution.py:422

commit v7 on v6

--- a/solution.py
+++ b/solution.py
@@ -271,18 +271,16 @@
             value = jnp.where(panel_lanes < PANEL, block, unit)
         else:
             value = panel[...]
-        for j in range(piece * CHOL, (piece + 1) * CHOL, 2):
-            first = jnp.broadcast_to(value[:, j : j + 1], (PANEL, LANES))
-            second = jnp.broadcast_to(value[:, j + 1 : j + 2], (PANEL, LANES))
-            ratio = first[j + 1 : j + 2, :] / first[j : j + 1, :]
-            top = value[j : j + 1, :]
-            next_row = value[j + 1 : j + 2, :] - ratio * top
-            pivot = second[j + 1 : j + 2, :] - ratio * first[j + 1 : j + 2, :]
-            change = first * (top / first[j : j + 1, :]) + (second - first * ratio) * (
-                next_row / pivot
-            )
-            value = jnp.where(panel_rows > j + 1, value - change, value)
-            value = jnp.where(panel_rows == j + 1, next_row, value)
+        tiles = value.reshape(PANEL // TILE, TILE, LANES)
+        tile_rows = panel_rows.reshape(PANEL // TILE, TILE, LANES)
+        for j in range(piece * CHOL, (piece + 1) * CHOL):
+            column = jnp.broadcast_to(tiles[:, :, j : j + 1], tiles.shape)
+            here_j = (j // TILE, slice(j % TILE, j % TILE + 1))
+            pivot = jnp.broadcast_to(column[here_j], (TILE, LANES))
+            row = jnp.broadcast_to(tiles[here_j], (TILE, LANES))
+            below = jnp.where(tile_rows > j, column, 0.0)
+            tiles = tiles - below * (row * (1.0 / pivot))[None]
+        value = tiles.reshape(PANEL, LANES)
         panel[...] = value
         if (piece + 1) * CHOL < PANEL:
             return

time: 78.6 us -> 80.1 us (1.019)
  Pallas kernels: 77.8 us -> 79.3 us
    pallas_call x1, Pallas kernels: 73.7 us -> 75.2 us  [per_device(): pl.pallas_call(functools.partial(sum_kernel, rows, cols), out_shape=(jax....]
where the time goes in v7:
time: 80.1 us; the launch traced here: 79.9 us
  Pallas kernels  79.3 us (99%)
    pallas_call x1, Pallas kernels, per_device(): pl.pallas_call(functools.partial(sum_kernel, rows, cols), out_shape=(jax....  75.2 us
    pallas_call x1, Pallas kernels, per_device(): pl.pallas_call(hand_over, out_shape=(jax.ShapeDtypeStruct((height, rank),...  4.14 us

profile of v7, /device:TPU:1, one launch (start us, length us, event | category | flops | bytes accessed | tf_op | source)
XLA Modules:
  0.0 79.9 jit_solution(2407225414370639943)
XLA Ops:
  0.6 75.2 %shard_map.41 = (f32[512,128]{1,0:T(8,128)}, f32[128,8192]{1,0:T(8,128)}) custom-call(f32[512,8192]{1,0:T(8,128)} %slab.1, f32[8192,128]{1,0:T(8,128)} %sketch.1), custom_call_target="tpu_custom_call" | custom-call | tf_op jit(solution)/shard_map/pallas_call | solution.py:382
  75.8 4.1 %shard_map.42 = (f32[512,128]{1,0:T(8,128)}, f32[128,8192]{1,0:T(8,128)}) custom-call(f32[512,128]{1,0:T(8,128)} %get-tuple-element.4.basis, f32[128,8192]{1,0:T(8,128)} %get-tuple-element.5.projection), custom_call_target="tpu_custom_call" | custom-call | tf_op jit(solution)/shard_map/pallas_call | solution.py:420

commit v8 on v6

--- a/solution.py
+++ b/solution.py
@@ -16,6 +16,8 @@
 LOAD = 1024
 CHUNKS = 8
 STRIP = 512
+PIECE = 16
+MOST_PIECES = 4
 SPACING = 2
 GRAM_HOP = 2
 PANEL = 32
@@ -67,8 +69,9 @@
     chunk_cols = width // chunks
     loads = width // LOAD
 
-    sketch_copy = pltpu.make_async_copy(sketch, sk, sk_sem)
-    sketch_copy.start()
+    def load_sketch(i):
+        band = pl.ds(i * LOAD, LOAD)
+        return pltpu.make_async_copy(sketch.at[band], sk.at[band], sk_sem.at[i])
 
     def load(i):
         return pltpu.make_async_copy(
@@ -76,6 +79,7 @@
         )
 
     for i in range(loads):
+        load_sketch(i).start()
         load(i).start()
 
     halving, swapping = orders(rows, cols)
@@ -88,21 +92,23 @@
         pl.semaphore_signal(barrier, inc=1, device_id=device, device_id_type=MESH)
 
     wide_acc[...] = jnp.zeros_like(wide_acc)
-    sketch_copy.wait()
-
-    def sample(i, carry):
-        load(i).wait()
-        a_high, a_low = split(staged[i])
-        columns = pl.ds(pl.multiple_of(i * LOAD, LOAD), LOAD)
-        high[:, columns] = a_high
-        low[:, columns] = a_low
+
+    def multiply(i):
+        columns = slice(i * LOAD, (i + 1) * LOAD)
         s_high, s_low = split(sk[columns, :])
         both = jnp.concatenate([s_high, s_low], axis=1)
-        wide_acc[...] += jnp.dot(a_high, both, preferred_element_type=F32)
-        wide_acc[:, :LANES] += jnp.dot(a_low, s_high, preferred_element_type=F32)
-        return carry
-
-    lax.fori_loop(0, loads, sample, 0)
+        wide_acc[...] += jnp.dot(high[:, columns], both, preferred_element_type=F32)
+        wide_acc[:, :LANES] += jnp.dot(low[:, columns], s_high, preferred_element_type=F32)
+
+    for i in range(loads + 1):
+        if i < loads:
+            load_sketch(i).wait()
+            load(i).wait()
+            columns = slice(i * LOAD, (i + 1) * LOAD)
+            high[:, columns], low[:, columns] = split(staged[i])
+        if i:
+            multiply(i - 1)
+
     sampled = wide_acc[:, :LANES] + wide_acc[:, LANES:]
     basis[...] = sampled
     turned = sampled.T
@@ -150,33 +156,52 @@
         return pltpu.make_async_remote_copy(
             src_ref=source,
             dst_ref=swap_in.at[k, s],
-            send_sem=send_sem.at[k, halves + s],
-            recv_sem=recv_sem.at[k, halves + s],
+            send_sem=send_sem.at[k, halves + s, 0],
+            recv_sem=recv_sem.at[k, halves + s, 0],
             device_id=pick(*swapping[s])[0],
             device_id_type=MESH,
         )
 
+    class Pieces:
+        def __init__(self, copies):
+            self.copies = copies
+
+        def start(self):
+            for copy in self.copies:
+                copy.start()
+
+        def wait_recv(self):
+            for copy in self.copies:
+                copy.wait_recv()
+
+        def wait_send(self):
+            for copy in self.copies:
+                copy.wait_send()
+
+    def cut(device, source, source_at, target, target_at, size, k, index):
+        pieces = min(MOST_PIECES, max(1, size // PIECE))
+        each = size // pieces
+        return Pieces(
+            [
+                pltpu.make_async_remote_copy(
+                    src_ref=source.at[pl.ds(source_at + p * each, each)],
+                    dst_ref=target.at[pl.ds(target_at + p * each, each)],
+                    send_sem=send_sem.at[k, index, p],
+                    recv_sem=recv_sem.at[k, index, p],
+                    device_id=device,
+                    device_id_type=MESH,
+                )
+                for p in range(pieces)
+            ]
+        )
+
     def scatter(k, s):
         device, _, give, half, slot = place(k, s)
-        return pltpu.make_async_remote_copy(
-            src_ref=part.at[pl.ds(give, half)],
-            dst_ref=landed.at[pl.ds(slot, half)],
-            send_sem=send_sem.at[k, s],
-            recv_sem=recv_sem.at[k, s],
-            device_id=device,
-            device_id_type=MESH,
-        )
+        return cut(device, part, give, landed, slot, half, k, s)
 
     def gather(k, s):
         device, keep, _, half, _ = place(k, s)
-        return pltpu.make_async_remote_copy(
-            src_ref=total.at[pl.ds(keep, half)],
-            dst_ref=total.at[pl.ds(keep, half)],
-            send_sem=send_sem.at[k, 2 * halves + swaps - 1 - s],
-            recv_sem=recv_sem.at[k, 2 * halves + swaps - 1 - s],
-            device_id=device,
-            device_id_type=MESH,
-        )
+        return cut(device, total, keep, total, keep, half, k, 2 * halves + swaps - 1 - s)
 
     def exchange_gram(s):
         device, _ = pick(*gram_order[s])
@@ -407,9 +432,9 @@
             pltpu.VMEM((PANEL, rank), F32),
             pltpu.VMEM((height, 2 * rank), F32),
             pltpu.SemaphoreType.DMA((width // LOAD,)),
-            pltpu.SemaphoreType.DMA,
-            pltpu.SemaphoreType.DMA((CHUNKS, 2 * halves + swaps)),
-            pltpu.SemaphoreType.DMA((CHUNKS, 2 * halves + swaps)),
+            pltpu.SemaphoreType.DMA((width // LOAD,)),
+            pltpu.SemaphoreType.DMA((CHUNKS, 2 * halves + swaps, MOST_PIECES)),
+            pltpu.SemaphoreType.DMA((CHUNKS, 2 * halves + swaps, MOST_PIECES)),
             pltpu.SemaphoreType.DMA((bits,)),
             pltpu.SemaphoreType.DMA((bits,)),
             pltpu.SemaphoreType.DMA((CHUNKS,)),

time: 78.6 us -> 81.4 us (1.036)
  Pallas kernels: 77.8 us -> 80.6 us
    pallas_call x1, Pallas kernels: 73.7 us -> 76.5 us  [per_device(): pl.pallas_call(functools.partial(sum_kernel, rows, cols), out_shape=(jax....]
where the time goes in v8:
time: 81.4 us; the launch traced here: 81.2 us
  Pallas kernels  80.6 us (99%)
    pallas_call x1, Pallas kernels, per_device(): pl.pallas_call(functools.partial(sum_kernel, rows, cols), out_shape=(jax....  76.5 us
    pallas_call x1, Pallas kernels, per_device(): pl.pallas_call(hand_over, out_shape=(jax.ShapeDtypeStruct((height, rank),...  4.14 us

profile of v8, /device:TPU:1, one launch (start us, length us, event | category | flops | bytes accessed | tf_op | source)
XLA Modules:
  0.0 81.2 jit_solution(2102088699530143806)
XLA Ops:
  0.6 76.5 %shard_map.41 = (f32[512,128]{1,0:T(8,128)}, f32[128,8192]{1,0:T(8,128)}) custom-call(f32[512,8192]{1,0:T(8,128)} %slab.1, f32[8192,128]{1,0:T(8,128)} %sketch.1), custom_call_target="tpu_custom_call" | custom-call | tf_op jit(solution)/shard_map/pallas_call | solution.py:409
  77.1 4.1 %shard_map.42 = (f32[512,128]{1,0:T(8,128)}, f32[128,8192]{1,0:T(8,128)}) custom-call(f32[512,128]{1,0:T(8,128)} %get-tuple-element.4.basis, f32[128,8192]{1,0:T(8,128)} %get-tuple-element.5.projection), custom_call_target="tpu_custom_call" | custom-call | tf_op jit(solution)/shard_map/pallas_call | solution.py:447

commit v9 on v6

--- a/solution.py
+++ b/solution.py
@@ -13,13 +13,13 @@
 F32 = jnp.float32
 LANES = 128
 TILE = 8
-LOAD = 1024
-CHUNKS = 8
+LOAD = 2048
+CHUNKS = 4
 STRIP = 512
 SPACING = 2
 GRAM_HOP = 2
 PANEL = 32
-CHOL = 8
+CHOL = 16
 
 
 def split(value):

time: 78.6 us -> 72.2 us (0.919)
  Pallas kernels: 77.8 us -> 71.4 us
    pallas_call x1, Pallas kernels: 73.7 us -> 67.3 us  [per_device(): pl.pallas_call(functools.partial(sum_kernel, rows, cols), out_shape=(jax....]
where the time goes in v9:
time: 72.2 us; the launch traced here: 72 us
  Pallas kernels  71.4 us (99%)
    pallas_call x1, Pallas kernels, per_device(): pl.pallas_call(functools.partial(sum_kernel, rows, cols), out_shape=(jax....  67.3 us
    pallas_call x1, Pallas kernels, per_device(): pl.pallas_call(hand_over, out_shape=(jax.ShapeDtypeStruct((height, rank),...  4.14 us

profile of v9, /device:TPU:1, one launch (start us, length us, event | category | flops | bytes accessed | tf_op | source)
XLA Modules:
  0.0 72.0 jit_solution(1366075312383533598)
XLA Ops:
  0.6 67.3 %shard_map.41 = (f32[512,128]{1,0:T(8,128)}, f32[128,8192]{1,0:T(8,128)}) custom-call(f32[512,8192]{1,0:T(8,128)} %slab.1, f32[8192,128]{1,0:T(8,128)} %sketch.1), custom_call_target="tpu_custom_call" | custom-call | tf_op jit(solution)/shard_map/pallas_call | solution.py:384
  67.9 4.1 %shard_map.42 = (f32[512,128]{1,0:T(8,128)}, f32[128,8192]{1,0:T(8,128)}) custom-call(f32[512,128]{1,0:T(8,128)} %get-tuple-element.4.basis, f32[128,8192]{1,0:T(8,128)} %get-tuple-element.5.projection), custom_call_target="tpu_custom_call" | custom-call | tf_op jit(solution)/shard_map/pallas_call | solution.py:422
